TPU v7x, 32 devices: a whole 2x2x4 slice. The times are simulated.
32 devices in a mesh: chan: 8 (over z, x), tile: 4 (over y, core).
Axes of the slice: x: 2, y: 2, z: 4, core: 2. Of those that a mesh axis runs over, the one named last changes fastest.
Arguments:
- voltage: float32 [2, 64, 512, 1024], P(None, 'tile', 'chan'), may hold values from -6 to 6
- fir_taps: float32 [4, 1024], replicated, may hold values from -3 to 3
- tile_slot: int32 [10], replicated, may hold values from 0 to 11, as said below
- tile_blocks: int32 [10, 2], replicated, may hold values from 0 to 3, as said below
Outputs:
- visibility: float32 [12, 1024, 2, 128, 128], P('tile', 'chan')
Inputs may be any that keep to these rules, and one draw needn't show every extreme that they name: `tile_slot`: the values are distinct; slot g belongs to device g // 3 of the tile axis. Every device of the tile axis holds at least one tile and at most 3, some exactly 3, and a device's tiles fill its lowest slots. `tile_blocks`: the unordered pairs of the rows are the 10 pairs of blocks p <= q, each once; a row may name its pair in either order.
All inputs are finite; a program needn't handle non-finite values.
Results may differ from a plain program's by a relative error of at most 0.0001.
Values sent between devices are 32-bit elements; how exact they have to be, the bound alone decides.
No kernel may reach another device: no remote copies, remote signals or barrier semaphores. Data moves between devices by JAX's collectives and lax.ppermute only.
A program may use at most 256 MiB of HBM per device.

v0:
```python
import functools
import math

import jax
import jax.numpy as jnp
import numpy as np
from jax import lax
from jax.experimental import pallas as pl
from jax.experimental.pallas import tpu as pltpu
from jax.sharding import PartitionSpec as P

BLOCK = 128
RADIX = 4
STEP = 256
LONG = 2_000_000_000_000
VMEM_BYTES = 14 * 1024 * 1024
BF16 = jnp.bfloat16
F32 = jnp.float32


def shifted(value, axis, steps):
    count = lax.axis_size(axis)
    initial, last = (max(0, -steps), min(count, count - steps))
    return lax.ppermute(value, axis, [(source, source + steps) for source in range(initial, last)])


def swapped(value, axis, mask):
    count = lax.axis_size(axis)
    return lax.ppermute(value, axis, [(source, source ^ mask) for source in range(count)])


def params():
    return pltpu.CompilerParams(vmem_limit_bytes=VMEM_BYTES)


def split(value):
    high = value.astype(BF16)
    return high, (value - high.astype(F32)).astype(BF16)


def filter_frames(voltage, fir_taps):
    tap_count = fir_taps.shape[0]
    frames = voltage.shape[1]
    history = shifted(voltage[:, : tap_count - 1], "tile", -1)
    extended = jnp.concatenate([voltage, history], axis=1)
    filtered = jnp.zeros(voltage.shape, jnp.float32)
    for tap_index in range(tap_count):
        filtered = (
            filtered
            + fir_taps[tap_index][None, None, None, :] * extended[:, tap_index : tap_index + frames]
        )
    return filtered


def transform(filtered):
    channel_count = filtered.shape[3]
    row_count = filtered.shape[1] * filtered.shape[2]
    position = lax.broadcasted_iota(jnp.int32, (channel_count, channel_count), 0)
    frequency = lax.broadcasted_iota(jnp.int32, (channel_count, channel_count), 1)
    phase_angle = (position * frequency % channel_count).astype(jnp.float32) * (
        2.0 * math.pi / channel_count
    )
    factor = 1.0 / math.sqrt(channel_count)
    cosine = jnp.cos(phase_angle) * factor
    sine_table = jnp.sin(phase_angle) * factor
    samples = filtered.reshape(2 * row_count, channel_count)
    cos_part = jnp.dot(
        cosine, samples.T, precision=lax.Precision.HIGHEST, preferred_element_type=jnp.float32
    )
    sin_part = jnp.dot(
        sine_table, samples.T, precision=lax.Precision.HIGHEST, preferred_element_type=jnp.float32
    )
    real_part = cos_part[:, :row_count] + sin_part[:, row_count:]
    imag_part = cos_part[:, row_count:] - sin_part[:, :row_count]
    joined = jnp.concatenate([real_part, imag_part], axis=1)
    return joined.reshape(channel_count, 2, filtered.shape[1], filtered.shape[2])


def tile_product(gathered, row_block, col_block, block_width):
    left_block = lax.dynamic_slice_in_dim(gathered, row_block * block_width, block_width, 3)
    right_block = lax.dynamic_slice_in_dim(gathered, col_block * block_width, block_width, 3)
    channel_count = gathered.shape[0]
    depth = 2 * gathered.shape[2]
    left_real = left_block.reshape(channel_count, depth, block_width)
    left_imag = jnp.concatenate([left_block[:, 1], -left_block[:, 0]], axis=1)
    left_both = jnp.concatenate([left_real, left_imag], axis=2)
    right_both = right_block.reshape(channel_count, depth, block_width)
    return jnp.einsum(
        "cki,ckj->cij",
        left_both,
        right_both,
        precision=lax.Precision.HIGHEST,
        preferred_element_type=jnp.float32,
    )


def own_slots(tile_slot, tile_blocks, slot_count):
    first_slot = lax.axis_index("tile") * slot_count
    row_blocks = []
    col_blocks = []
    present = []
    for slot_index in range(slot_count):
        matches = (tile_slot == first_slot + slot_index).astype(jnp.int32)
        row_blocks.append(jnp.sum(matches * tile_blocks[:, 0]))
        col_blocks.append(jnp.sum(matches * tile_blocks[:, 1]))
        present.append(jnp.sum(matches))
    return row_blocks, col_blocks, present


def generic_body(voltage, fir_taps, tile_slot, tile_blocks):
    spectra = transform(filter_frames(voltage, fir_taps))
    tile_count = tile_blocks.shape[0]
    tile_size = lax.axis_size("tile")
    slot_count = (tile_count + tile_size - 1) // tile_size
    turned = lax.all_to_all(spectra, "chan", split_axis=0, concat_axis=3, tiled=True)
    spectra_total = turned.shape[2] * tile_size
    row_blocks, col_blocks, present = own_slots(tile_slot, tile_blocks, slot_count)
    portion = lax.all_gather(turned, "tile", axis=2, tiled=True)
    summed = jnp.stack(
        [
            tile_product(portion, row_blocks[slot_index], col_blocks[slot_index], BLOCK)
            for slot_index in range(slot_count)
        ]
    )
    weights = jnp.stack(present).astype(F32)[:, None, None, None] / spectra_total
    return (summed * weights).reshape(slot_count, turned.shape[0], 2, BLOCK, BLOCK)


def fourier_table(points, owners, scale):
    phase = np.outer(np.arange(points), np.arange(points)) % points
    angle = phase * (2.0 * math.pi / points)
    cosine = np.cos(angle) * scale
    sine = np.sin(angle) * scale
    both = np.stack([np.concatenate([cosine, sine], 1), np.concatenate([-sine, cosine], 1)], 0)
    both = both.reshape(2, owners, points // owners, 2 * points).transpose(1, 0, 2, 3)
    return both.reshape(owners, -1, 2 * points).astype(np.float32)


def twiddle_table(length):
    angle = np.outer(np.arange(1, RADIX), np.arange(length // RADIX)) * (2.0 * math.pi / length)
    return np.stack([np.cos(angle), np.sin(angle)], 1).reshape(-1, length // RADIX).astype(np.float32)


def filter_kernel(frames, voltage_ref, next_ref, taps_ref, twiddle_ref, *refs):
    out_refs = refs[-2 * RADIX :]
    tap_count, length = taps_ref.shape
    held = voltage_ref.shape[1]
    points = length // RADIX

    def quarter(part, frame, index):
        lanes = slice(index * points, (index + 1) * points)
        total = None
        for tap in range(tap_count):
            at = frame + tap
            source = voltage_ref[part, at, :, lanes] if at < held else next_ref[part, at - held, :, lanes]
            term = source * taps_ref[pl.ds(tap, 1), lanes]
            total = term if total is None else total + term
        return total

    for frame in range(frames):
        real = [quarter(0, frame, index) for index in range(RADIX)]
        imag = [quarter(1, frame, index) for index in range(RADIX)]
        even_real, odd_real = real[0] + real[2], real[1] + real[3]
        even_imag, odd_imag = imag[0] + imag[2], imag[1] + imag[3]
        left_real, right_real = real[0] - real[2], real[1] - real[3]
        left_imag, right_imag = imag[0] - imag[2], imag[1] - imag[3]
        residues = [
            (even_real + odd_real, even_imag + odd_imag),
            (left_real + right_imag, left_imag - right_real),
            (even_real - odd_real, even_imag - odd_imag),
            (left_real - right_imag, left_imag + right_real),
        ]
        for index, (re, im) in enumerate(residues):
            if index:
                cosine = twiddle_ref[pl.ds(2 * index - 2, 1), :]
                sine = twiddle_ref[pl.ds(2 * index - 1, 1), :]
                re, im = re * cosine + im * sine, im * cosine - re * sine
            for part, value in enumerate((re, im)):
                high, low = split(value)
                lanes = slice(part * points, (part + 1) * points)
                out_refs[2 * index][frame, :, lanes] = high
                out_refs[2 * index + 1][frame, :, lanes] = low


def filtered_samples(voltage, following, fir_taps, late, earlier, after):
    _, frames, inputs, length = voltage.shape
    width = 16
    depth = 2 * length // RADIX
    twiddles = jnp.asarray(twiddle_table(length))
    out = jax.ShapeDtypeStruct((frames, inputs, depth), BF16)
    if earlier:
        count, held, place = late, late, frames // late - 1
    else:
        count, held, place = frames - late, frames, 0
    others = list(earlier) + list(after)
    return pl.pallas_call(
        functools.partial(filter_kernel, count),
        grid=(inputs // width,),
        in_specs=[
            pl.BlockSpec((2, held, width, length), lambda i: (0, place, i, 0)),
            pl.BlockSpec((2, following.shape[1], width, length), lambda i: (0, 0, i, 0)),
            pl.BlockSpec(fir_taps.shape, lambda i: (0, 0)),
            pl.BlockSpec(twiddles.shape, lambda i: (0, 0)),
        ]
        + [pl.BlockSpec(memory_space=pl.ANY)] * len(others),
        out_specs=[pl.BlockSpec((count, width, depth), lambda i: (place, i, 0))] * (2 * RADIX),
        out_shape=[out] * (2 * RADIX),
        input_output_aliases={4 + index: index for index in range(len(earlier))},
        compiler_params=params(),
        cost_estimate=pl.CostEstimate(
            flops=16 * voltage.size * count // frames,
            bytes_accessed=8 * voltage.size * count // frames,
            transcendentals=0,
        ),
        name="filter",
    )(voltage, following, fir_taps, twiddles, *others)


def dot_rows(left, right):
    return lax.dot_general(left, right, (((1,), (1,)), ((), ())), preferred_element_type=F32)


def transform_kernel(groups, pieces, table_ref, xh_ref, xl_ref, *refs):
    out_refs, (th_ref, tl_ref) = refs[-2 - len(groups) * pieces : -2], refs[-2:]
    height = table_ref.shape[1]
    masks = [mask for group in groups for mask in group]

    @pl.when(pl.program_id(0) == 0)
    def _():
        me = lax.axis_index("chan")
        for index, mask in enumerate(masks):
            rows = slice(index * height, (index + 1) * height)
            th_ref[rows], tl_ref[rows] = split(table_ref[me ^ mask])

    high = xh_ref[...]
    result = dot_rows(th_ref[...], high) + dot_rows(th_ref[...], xl_ref[...])
    result = result + dot_rows(tl_ref[...], high)
    count = height // 2
    size = count // pieces
    places = [(which, at) for which, group in enumerate(groups) for at in range(len(group))]
    for index, (which, at) in enumerate(places):
        for part in range(2):
            for piece in range(pieces):
                first = index * height + part * count + piece * size
                for column in range(result.shape[1] // BLOCK):
                    out_refs[which * pieces + piece][at, part, column] = result[
                        first : first + size, column * BLOCK : (column + 1) * BLOCK
                    ]


def transformed(groups, pieces, table, samples, after, first, last, work):
    depth = samples[0].shape[1]
    owners, height, _ = table.shape
    size = height // 2 // pieces
    step = STEP
    rows = (last - first) * step
    row_spec = pl.BlockSpec((step, depth), lambda i: (first + i, 0))
    total = sum(map(len, groups)) * height
    counts = [len(group) for group in groups for _ in range(pieces)]
    return pl.pallas_call(
        functools.partial(transform_kernel, groups, pieces),
        grid=(rows // step,),
        in_specs=[pl.BlockSpec(table.shape, lambda i: (0, 0, 0)), row_spec, row_spec]
        + [pl.BlockSpec(memory_space=pl.ANY)] * len(after),
        out_specs=[
            pl.BlockSpec((count, 2, step // BLOCK, size, BLOCK), lambda i: (0, 0, i, 0, 0))
            for count in counts
        ],
        out_shape=[
            jax.ShapeDtypeStruct((count, 2, rows // BLOCK, size, BLOCK), F32) for count in counts
        ],
        scratch_shapes=[pltpu.VMEM((total, depth), BF16)] * 2,
        compiler_params=params(),
        cost_estimate=pl.CostEstimate(
            flops=work or 3 * 2 * total * depth * rows,
            bytes_accessed=4 * depth * rows + 4 * table.size + 4 * total * rows,
            transcendentals=0,
        ),
        name="transform",
    )(table, *samples, *after)


def merge_kernel(count, groups, piece, *refs):
    near_refs, far_refs, out_refs = refs[: len(groups)], refs[len(groups) : 2 * len(groups)], refs[-count:]
    total = sum(groups)
    odd = lax.axis_index("chan") % 2 == 1
    lower = lax.broadcasted_iota(jnp.int32, (total, BLOCK), 1) < BLOCK // 2
    for unit, out_ref in enumerate(out_refs):
        for channel in range(piece):
            for part in range(2):

                def rows_of(segment_refs):
                    rows = [
                        ref[pl.ds((unit * 2 + part) * held * piece + channel, held, stride=piece), :]
                        for ref, held in zip(segment_refs, groups)
                    ]
                    return rows[0] if len(rows) == 1 else jnp.concatenate(rows, axis=0)

                near, far = rows_of(near_refs), rows_of(far_refs)
                first = jnp.where(odd, far, near)
                second = jnp.where(odd, near, far)
                at = part * 2 * total
                out_ref[channel, at : at + total] = jnp.where(
                    lower, first, pltpu.roll(second, BLOCK // 2, 1)
                )
                out_ref[channel, at + total : at + 2 * total] = jnp.where(
                    lower, pltpu.roll(first, BLOCK // 2, 1), second
                )


def merged(near, far, after):
    count, _, _, piece, lanes = near[0].shape
    groups = [value.shape[2] for value in near]
    size = sum(value.size for value in near)
    return pl.pallas_call(
        functools.partial(merge_kernel, count, groups, piece),
        in_specs=[pl.BlockSpec(memory_space=pltpu.VMEM)] * (2 * len(near))
        + [pl.BlockSpec(memory_space=pl.ANY)] * len(after),
        out_specs=[pl.BlockSpec(memory_space=pltpu.VMEM)] * count,
        out_shape=[jax.ShapeDtypeStruct((piece, 4 * sum(groups), lanes), F32)] * count,
        compiler_params=params(),
        cost_estimate=pl.CostEstimate(flops=4 * size, bytes_accessed=16 * size, transcendentals=0),
        name="merge",
    )(*[value.reshape(-1, lanes) for value in list(near) + list(far)], *after)


def pack_kernel(counts, *refs):
    sources = iter(refs)
    for count, out_ref in zip(counts, refs[-len(counts) :]):
        for index in range(count):
            out_ref[index] = next(sources)[...]


def packed(batches, after, work=0):
    counts = [len(batch) for batch in batches]
    values = [value for batch in batches for value in batch]
    width = 8

    def spec(shape):
        lead = shape[:-3]
        return pl.BlockSpec(
            lead + (min(width, shape[-3]),) + shape[-2:], lambda i: (0,) * len(lead) + (i, 0, 0)
        )

    shapes = [(len(batch),) + batch[0].shape for batch in batches]
    return pl.pallas_call(
        functools.partial(pack_kernel, counts),
        grid=(values[0].shape[-3] // min(width, values[0].shape[-3]),),
        in_specs=[spec(value.shape) for value in values]
        + [pl.BlockSpec(memory_space=pl.ANY)] * len(after),
        out_specs=[spec(shape) for shape in shapes],
        out_shape=[jax.ShapeDtypeStruct(shape, F32) for shape in shapes],
        compiler_params=params(),
        cost_estimate=pl.CostEstimate(
            flops=work,
            bytes_accessed=8 * sum(value.size for value in values),
            transcendentals=0,
        ),
        name="pack",
    )(*values, *after)


def dot_columns(left, right):
    return lax.dot_general(left, right, (((0,), (0,)), ((), ())), preferred_element_type=F32)


def correlate_kernel(slots, tiles, order, slot_ref, blocks_ref, *refs):
    unit_refs = []
    for ref in refs[:-5]:
        if len(ref.shape) == 4:
            unit_refs.append(ref)
        elif len(ref.shape) == 5:
            unit_refs += [ref.at[0], ref.at[1]]
    near_refs = unit_refs[tiles:]
    out_ref, done_ref, high_ref, low_ref, place_ref = refs[-5:]
    done_ref[...] = jnp.zeros(done_ref.shape, F32)
    far, width, depth, _ = unit_refs[0].shape
    blocks = far + 1
    rows = depth // 2
    half = tiles * rows

    @pl.when(pl.program_id(0) == 0)
    def _():
        first_slot = lax.axis_index("tile") * slots
        for slot in range(slots):
            row = jnp.int32(0)
            col = jnp.int32(0)
            present = jnp.int32(0)
            for tile in range(slot_ref.shape[0]):
                match = (slot_ref[tile] == first_slot + slot).astype(jnp.int32)
                row = row + match * blocks_ref[2 * tile]
                col = col + match * blocks_ref[2 * tile + 1]
                present = present + match
            place_ref[3 * slot] = row
            place_ref[3 * slot + 1] = col
            place_ref[3 * slot + 2] = present

    own = lax.axis_index("chan") // 2
    for channel in range(width):
        for mask in range(blocks):
            block = own ^ order[mask]
            for part in range(2):
                joined = jnp.concatenate(
                    [
                        (unit_refs[tile][mask, channel, part * rows : (part + 1) * rows])
                        if mask < far
                        else near_refs[tile][0, channel, part * rows : (part + 1) * rows]
                        for tile in range(tiles)
                    ],
                    axis=0,
                )
                high, low = split(joined)
                high_ref[channel, block, part * half : (part + 1) * half] = high
                low_ref[channel, block, part * half : (part + 1) * half] = low
        for slot in range(slots):
            row = place_ref[3 * slot]
            col = place_ref[3 * slot + 1]
            weight = place_ref[3 * slot + 2].astype(F32)
            row_high = high_ref[channel, row]
            row_low = low_ref[channel, row]
            col_high = high_ref[channel, col]
            col_low = low_ref[channel, col]
            turned_high = jnp.concatenate([-col_high[half:], col_high[:half]], axis=0)
            turned_low = jnp.concatenate([-col_low[half:], col_low[:half]], axis=0)
            right_high = jnp.concatenate([col_high, turned_high], axis=1)
            right_low = jnp.concatenate([col_low, turned_low], axis=1)
            value = dot_columns(
                jnp.concatenate([row_high, row_low], axis=0),
                jnp.concatenate([right_high, right_high], axis=0),
            ) + dot_columns(row_high, right_low)
            value = value * weight
            out_ref[slot, channel, 0] = value[:, :BLOCK]
            out_ref[slot, channel, 1] = value[:, BLOCK:]


def correlated(order, tile_slot, tile_blocks, units, before, visibility, residue, first, total, slots):
    tiles = sum(1 if unit.ndim == 4 else unit.shape[0] for unit in units)
    blocks = len(order)
    piece, depth, lanes = units[0].shape[-3:]
    width = 4
    out = jax.ShapeDtypeStruct((slots, total, RADIX, 2, BLOCK, BLOCK), F32)
    operands = [tile_slot, tile_blocks.reshape(-1)] + units + before

    def spec(unit, held, at):
        lead = unit.shape[:-4]
        return pl.BlockSpec(
            lead + (held, width, depth, lanes), lambda i, *_: (0,) * len(lead) + (at, i, 0, 0)
        )

    in_specs = [spec(unit, blocks - 1, 0) for unit in units]
    in_specs += [spec(unit, 1, unit.shape[-4] - 1) for unit in before]
    aliases = {}
    if visibility is not None:
        operands.append(visibility)
        in_specs.append(pl.BlockSpec(memory_space=pl.ANY))
        aliases = {len(operands) - 1: 0}
    return pl.pallas_call(
        functools.partial(correlate_kernel, slots, tiles, order),
        grid_spec=pltpu.PrefetchScalarGridSpec(
            num_scalar_prefetch=2,
            grid=(piece // width,),
            in_specs=in_specs,
            out_specs=[
                pl.BlockSpec(
                    (slots, width, None, 2, BLOCK, BLOCK), lambda i, *_: (0, first // width + i, residue, 0, 0, 0)
                ),
                pl.BlockSpec((8, BLOCK), lambda i, *_: (0, 0)),
            ],
            scratch_shapes=[pltpu.VMEM((width, blocks, tiles * depth, lanes), BF16)] * 2
            + [pltpu.SMEM((3 * slots,), jnp.int32)],
        ),
        out_shape=[out, jax.ShapeDtypeStruct((8, BLOCK), F32)],
        input_output_aliases=aliases,
        compiler_params=params(),
        cost_estimate=pl.CostEstimate(
            flops=3 * 2 * slots * piece * tiles * depth * BLOCK * 2 * BLOCK,
            bytes_accessed=4 * piece * lanes * (tiles * blocks * depth + slots * 2 * BLOCK),
            transcendentals=0,
        ),
        name="correlate",
    )(*operands)


def body(voltage, fir_taps, tile_slot, tile_blocks):
    _, frames, inputs, length = voltage.shape
    tap_count = fir_taps.shape[0]
    owners = lax.axis_size("chan")
    tiles = lax.axis_size("tile")
    channels = length // owners
    blocks = owners // 2
    slots = -(-tile_blocks.shape[0] // tiles)
    scale = 1.0 / math.sqrt(length * frames * tiles)
    table = jnp.asarray(fourier_table(length // RADIX, owners, scale))

    order = list(range(2, blocks)) + [1, 0]
    groups = [tuple(2 * block + x for block in order) for x in range(2)]
    halves = 2
    size = channels // RADIX // halves
    count = RADIX * halves
    near = [[] for _ in range(count)]
    share = [[] for _ in range(count)]
    away = [None] * count
    units = [None] * count
    paired = [None] * count

    steps = frames * inputs // STEP
    late = STEP // inputs
    following = shifted(voltage[:, : tap_count - 1], "tile", -1)
    early = filtered_samples(voltage, voltage[:, : tap_count - 1], fir_taps, late, [], [])

    def spectra(samples, residue, after, first, last, work=0):
        rows = [value.reshape(frames * inputs, -1) for value in samples[2 * residue : 2 * residue + 2]]
        values = transformed(groups, halves, table, rows, after, first, last, work)
        for half in range(halves):
            near[residue * halves + half].append(values[half])
            share[residue * halves + half].append(values[halves + half])

    spectra(early, 0, [], 0, steps - 1)
    samples = filtered_samples(voltage, following, fir_taps, late, early, [near[0][0]])
    spectra(samples, 0, [], steps - 1, steps)
    spectra(samples, 1, [], 0, steps)

    def leave(piece):
        values = share[piece]
        if 0 < piece < 5:
            after = [away[piece - 1][-1]]
            values = [packed([[value]], after)[0].reshape(value.shape) for value in values]
        away[piece] = [swapped(value, "chan", 1) for value in values]

    def merge(piece, after):
        units[piece] = merged(near[piece], away[piece], after)

    def along(piece):
        return [
            swapped(unit, "chan", 2 * block) if block else unit
            for block, unit in zip(order, units[piece])
        ]

    leave(0)
    merge(0, near[halves][:1])
    turned = along(0)
    for residue in range(2, RADIX):
        spectra(samples, residue, units[0][:1], 0, steps, LONG)
    leave(1)
    merge(1, [])
    leave(2)

    def products(piece, arrays, before, visibility):
        return correlated(
            order, tile_slot, tile_blocks, arrays, before, visibility,
            piece // halves, piece % halves * size, channels // RADIX, slots,
        )

    (seed,) = packed([list(units[0][-1:])], [])
    seed_across = swapped(seed, "tile", 2)
    (both,) = packed([[seed, seed_across]], [])
    before = [seed, seed_across, swapped(both, "tile", 1)]
    visibility = None
    finished = []
    pair = None
    for piece in range(count):
        if piece:
            after = [pair[1]]
            for later in range(piece + 1, min(piece + 3, count)):
                if units[later] is None:
                    merge(later, [])
                after.append(units[later][0])
        else:
            after = [units[1][0], away[2][0]] + [near[residue * halves][0] for residue in range(2, RADIX)]
            after += before[2:]
        after += finished[piece - 2 : piece - 1] if piece >= 2 else []
        following = list(units[piece + 1][-1:]) if piece + 1 < count else []
        (own,) = packed([turned[:-1] + following], after, LONG)
        if piece + 1 < count:
            turned = along(piece + 1)
        across = swapped(own, "tile", 2)
        if piece + 3 < count:
            leave(piece + 3)
        if pair:
            (both,) = packed([pair], [own] + (away[piece + 3][-1:] if piece + 3 < count else []))
            arrays = pair + [swapped(both, "tile", 1)]
            visibility, token = products(piece - 1, arrays, before, visibility)
            finished.append(token)
            before = arrays
        pair = [own, across]
    (last,) = packed([[across]], finished[-1:])
    arrays = pair + [swapped(own, "tile", 1), swapped(last[0], "tile", 1)]
    visibility, _ = products(count - 1, arrays, before, visibility)
    return visibility.reshape(slots, channels, 2, BLOCK, BLOCK)


def solution(mesh):
    in_specs = (P(None, "tile", "chan", None), P(), P(), P())
    out_specs = P("tile", "chan", None, None, None)
    owners, tiles = mesh.shape["chan"], mesh.shape["tile"]

    def run(voltage, fir_taps, tile_slot, tile_blocks):
        paired = 2 * voltage.shape[2] == BLOCK * owners and tiles == 4
        chosen = body if paired else generic_body
        return jax.shard_map(
            chosen, mesh=mesh, in_specs=in_specs, out_specs=out_specs, check_vma=False
        )(voltage, fir_taps, tile_slot, tile_blocks)

    return run
```

profile of v0, /device:TPU:13, one launch (start us, length us, event | category | flops | bytes accessed | tf_op | source)
XLA Modules:
  0.0 284.7 jit_solution(6307622234092456735)
XLA Ops:
  20.7 4.3 %collective-permute-done.1 = f32[4,2,6,16,128]{4,3,2,1,0:T(8,128)S(1)} collective-permute-done((f32[4,2,6,16,128]{4,3,2,1,0:T(8,128)S(1)}, f32[4,2,6,16,128]{4,3,2,1,0:T(8,128)S(1)}, u32[]{:S(2)}, u32[]{:S(2)}) %collective-permute-start.1) | collective-permute-done | bytes 393248 | tf_op jit(solution)/shard_map/ppermute | solution.py:29
  55.7 5.6 %collective-permute-done.33.refs_1_ = f32[16,32,128]{2,1,0:T(8,128)} collective-permute-done((f32[16,32,128]{2,1,0:T(8,128)}, f32[16,32,128]{2,1,0:T(8,128)}, u32[]{:S(2)}, u32[]{:S(2)}) %collective-permute-start.33) | collective-permute-done | bytes 262176 | tf_op jit(solution)/shard_map/ppermute | solution.py:29
  69.7 6.0 %collective-permute-done.17.refs_1_ = f32[4,2,8,16,128]{4,3,2,1,0:T(8,128)S(1)} collective-permute-done((f32[4,2,8,16,128]{4,3,2,1,0:T(8,128)S(1)}, f32[4,2,8,16,128]{4,3,2,1,0:T(8,128)S(1)}, u32[]{:S(2)}, u32[]{:S(2)}) %collective-permute-start.17) | collective-permute-done | bytes 524320 | tf_op jit(solution)/shard_map/ppermute | solution.py:29
  79.4 10.4 %collective-permute-done.30.refs_1_ = f32[16,32,128]{2,1,0:T(8,128)S(1)} collective-permute-done((f32[16,32,128]{2,1,0:T(8,128)S(1)}, f32[16,32,128]{2,1,0:T(8,128)S(1)}, u32[]{:S(2)}, u32[]{:S(2)}) %collective-permute-start.30) | collective-permute-done | bytes 262176 | tf_op jit(solution)/shard_map/ppermute | solution.py:29
  102.9 6.6 %correlate.8 = (f32[3,32,4,2,128,128]{5,4,3,2,1,0:T(8,128)}, f32[8,128]{1,0:T(8,128)S(1)}) custom-call(s32[10]{0:T(128)S(1)} %copy-done.37, s32[20]{0:T(128)S(1)} %reshape.118.blocks_ref, f32[4,16,32,128]{3,2,1,0:T(8,128)S(1)} %copy-done.12, f32[4,16,32,128]{3,2,1,0:T(8,128)S(1)} %copy-done.14, ...), custom_call_target="tpu_custom_call" | custom-call | flops 1207959552 | bytes 10485760 | tf_op jit(solution)/shard_map/correlate/pallas_call | solution.py:457
  112.3 7.8 %collective-permute-done.26.refs_1_ = f32[16,32,128]{2,1,0:T(8,128)} collective-permute-done((f32[16,32,128]{2,1,0:T(8,128)}, f32[16,32,128]{2,1,0:T(8,128)}, u32[]{:S(2)}, u32[]{:S(2)}) %collective-permute-start.26) | collective-permute-done | bytes 262176 | tf_op jit(solution)/shard_map/ppermute | solution.py:29
  129.0 6.3 %correlate.9 = (f32[3,32,4,2,128,128]{5,4,3,2,1,0:T(8,128)}, f32[8,128]{1,0:T(8,128)S(1)}) custom-call(s32[10]{0:T(128)S(1)} %copy-done.37, s32[20]{0:T(128)S(1)} %reshape.118.blocks_ref, f32[4,16,32,128]{3,2,1,0:T(8,128)S(1)} %pack.31.refs_2_.refs_0_.refs_3_, ...), custom_call_target="tpu_custom_call", output_to_operand_aliasing={{0}: (8, {})} | custom-call | flops 1207959552 | bytes 10485760 | tf_op jit(solution)/shard_map/correlate/pallas_call | solution.py:457
  135.2 4.6 %collective-permute-done.22.refs_0_ = f32[16,32,128]{2,1,0:T(8,128)S(1)} collective-permute-done((f32[16,32,128]{2,1,0:T(8,128)S(1)}, f32[16,32,128]{2,1,0:T(8,128)S(1)}, u32[]{:S(2)}, u32[]{:S(2)}) %collective-permute-start.22) | collective-permute-done | bytes 262176 | tf_op jit(solution)/shard_map/ppermute | solution.py:29
  139.8 7.4 %collective-permute-done.23.refs_1_ = f32[16,32,128]{2,1,0:T(8,128)S(1)} collective-permute-done((f32[16,32,128]{2,1,0:T(8,128)S(1)}, f32[16,32,128]{2,1,0:T(8,128)S(1)}, u32[]{:S(2)}, u32[]{:S(2)}) %collective-permute-start.23) | collective-permute-done | bytes 262176 | tf_op jit(solution)/shard_map/ppermute | solution.py:29
  155.5 5.3 %correlate.10 = (f32[3,32,4,2,128,128]{5,4,3,2,1,0:T(8,128)}, f32[8,128]{1,0:T(8,128)S(1)}) custom-call(s32[10]{0:T(128)S(1)} %copy-done.37, s32[20]{0:T(128)S(1)} %reshape.118.blocks_ref, f32[4,16,32,128]{3,2,1,0:T(8,128)S(1)} %pack.33.refs_2_.refs_0_.refs_3_, ...), custom_call_target="tpu_custom_call", output_to_operand_aliasing={{0}: (8, {})} | custom-call | flops 1207959552 | bytes 10485760 | tf_op jit(solution)/shard_map/correlate/pallas_call | solution.py:457
  160.8 5.3 %collective-permute-done.19.refs_0_ = f32[16,32,128]{2,1,0:T(8,128)S(1)} collective-permute-done((f32[16,32,128]{2,1,0:T(8,128)S(1)}, f32[16,32,128]{2,1,0:T(8,128)S(1)}, u32[]{:S(2)}, u32[]{:S(2)}) %collective-permute-start.19) | collective-permute-done | bytes 262176 | tf_op jit(solution)/shard_map/ppermute | solution.py:29
  166.1 7.8 %collective-permute-done.20.refs_1_ = f32[16,32,128]{2,1,0:T(8,128)S(1)} collective-permute-done((f32[16,32,128]{2,1,0:T(8,128)S(1)}, f32[16,32,128]{2,1,0:T(8,128)S(1)}, u32[]{:S(2)}, u32[]{:S(2)}) %collective-permute-start.20) | collective-permute-done | bytes 262176 | tf_op jit(solution)/shard_map/ppermute | solution.py:29
  182.2 5.3 %correlate.11 = (f32[3,32,4,2,128,128]{5,4,3,2,1,0:T(8,128)}, f32[8,128]{1,0:T(8,128)S(1)}) custom-call(s32[10]{0:T(128)S(1)} %copy-done.37, s32[20]{0:T(128)S(1)} %reshape.118.blocks_ref, f32[4,16,32,128]{3,2,1,0:T(8,128)S(1)} %copy-done.8, f32[4,16,32,128]{3,2,1,0:T(8,128)S(1)} %collective-permute-done.42.refs_4_.refs_1_, ...), custom_call_target="tpu_custom_call", output_to_operand_aliasing={{0}: (8, {})} | custom-call | flops 1207959552 | bytes 10485760 | tf_op jit(solution)/shard_map/correlate/pallas_call | solution.py:457
  187.4 6.6 %collective-permute-done.12.refs_0_ = f32[16,32,128]{2,1,0:T(8,128)S(1)} collective-permute-done((f32[16,32,128]{2,1,0:T(8,128)S(1)}, f32[16,32,128]{2,1,0:T(8,128)S(1)}, u32[]{:S(2)}, u32[]{:S(2)}) %collective-permute-start.12) | collective-permute-done | bytes 262176 | tf_op jit(solution)/shard_map/ppermute | solution.py:29
  194.0 7.8 %collective-permute-done.13.refs_1_ = f32[16,32,128]{2,1,0:T(8,128)S(1)} collective-permute-done((f32[16,32,128]{2,1,0:T(8,128)S(1)}, f32[16,32,128]{2,1,0:T(8,128)S(1)}, u32[]{:S(2)}, u32[]{:S(2)}) %collective-permute-start.13) | collective-permute-done | bytes 262176 | tf_op jit(solution)/shard_map/ppermute | solution.py:29
  208.3 5.3 %correlate.12 = (f32[3,32,4,2,128,128]{5,4,3,2,1,0:T(8,128)}, f32[8,128]{1,0:T(8,128)S(1)}) custom-call(s32[10]{0:T(128)S(1)} %copy-done.37, s32[20]{0:T(128)S(1)} %reshape.118.blocks_ref, f32[4,16,32,128]{3,2,1,0:T(8,128)S(1)} %copy-done.3, f32[4,16,32,128]{3,2,1,0:T(8,128)S(1)} %collective-permute-done.44.refs_4_.refs_1_, ...), custom_call_target="tpu_custom_call", output_to_operand_aliasing={{0}: (8, {})} | custom-call | flops 1207959552 | bytes 10485760 | tf_op jit(solution)/shard_map/correlate/pallas_call | solution.py:457
  213.5 5.3 %collective-permute-done.10.refs_2_ = f32[16,32,128]{2,1,0:T(8,128)S(1)} collective-permute-done((f32[16,32,128]{2,1,0:T(8,128)S(1)}, f32[16,32,128]{2,1,0:T(8,128)S(1)}, u32[]{:S(2)}, u32[]{:S(2)}) %collective-permute-start.10) | collective-permute-done | bytes 262176 | tf_op jit(solution)/shard_map/ppermute | solution.py:29
  218.9 10.4 %collective-permute-done.9.refs_1_ = f32[16,32,128]{2,1,0:T(8,128)S(1)} collective-permute-done((f32[16,32,128]{2,1,0:T(8,128)S(1)}, f32[16,32,128]{2,1,0:T(8,128)S(1)}, u32[]{:S(2)}, u32[]{:S(2)}) %collective-permute-start.9) | collective-permute-done | bytes 262176 | tf_op jit(solution)/shard_map/ppermute | solution.py:29
  234.7 5.3 %correlate.13 = (f32[3,32,4,2,128,128]{5,4,3,2,1,0:T(8,128)}, f32[8,128]{1,0:T(8,128)S(1)}) custom-call(s32[10]{0:T(128)S(1)} %copy-done.37, s32[20]{0:T(128)S(1)} %reshape.118.blocks_ref, f32[4,16,32,128]{3,2,1,0:T(8,128)S(1)} %pack.39.refs_2_.refs_0_.refs_3_, ...), custom_call_target="tpu_custom_call", output_to_operand_aliasing={{0}: (8, {})} | custom-call | flops 1207959552 | bytes 10485760 | tf_op jit(solution)/shard_map/correlate/pallas_call | solution.py:457
  239.9 7.9 %collective-permute-done.4.refs_0_ = f32[16,32,128]{2,1,0:T(8,128)S(1)} collective-permute-done((f32[16,32,128]{2,1,0:T(8,128)S(1)}, f32[16,32,128]{2,1,0:T(8,128)S(1)}, u32[]{:S(2)}, u32[]{:S(2)}) %collective-permute-start.4) | collective-permute-done | bytes 262176 | tf_op jit(solution)/shard_map/ppermute | solution.py:29
  247.8 7.8 %collective-permute-done.5.refs_1_ = f32[16,32,128]{2,1,0:T(8,128)S(1)} collective-permute-done((f32[16,32,128]{2,1,0:T(8,128)S(1)}, f32[16,32,128]{2,1,0:T(8,128)S(1)}, u32[]{:S(2)}, u32[]{:S(2)}) %collective-permute-start.5) | collective-permute-done | bytes 262176 | tf_op jit(solution)/shard_map/ppermute | solution.py:29
  261.0 5.3 %correlate.14 = (f32[3,32,4,2,128,128]{5,4,3,2,1,0:T(8,128)}, f32[8,128]{1,0:T(8,128)S(1)}) custom-call(s32[10]{0:T(128)S(1)} %copy-done.37, s32[20]{0:T(128)S(1)} %reshape.118.blocks_ref, f32[4,16,32,128]{3,2,1,0:T(8,128)S(1)} %pack.41.refs_2_.refs_0_.refs_4_, ...), custom_call_target="tpu_custom_call", output_to_operand_aliasing={{0}: (8, {})} | custom-call | flops 1207959552 | bytes 10485760 | tf_op jit(solution)/shard_map/correlate/pallas_call | solution.py:457
  266.3 10.1 %collective-permute-done.50.refs_0_.refs_1_ = f32[3,16,32,128]{3,2,1,0:T(8,128)S(1)} collective-permute-done((f32[3,16,32,128]{3,2,1,0:T(8,128)S(1)}, f32[3,16,32,128]{3,2,1,0:T(8,128)S(1)}, u32[]{:S(2)}, u32[]{:S(2)}) %collective-permute-start.50) | collective-permute-done | bytes 786464 | tf_op jit(solution)/shard_map/ppermute | solution.py:29
  279.4 5.3 %correlate.15 = (f32[3,32,4,2,128,128]{5,4,3,2,1,0:T(8,128)}, f32[8,128]{1,0:T(8,128)}) custom-call(s32[10]{0:T(128)S(1)} %copy-done.37, s32[20]{0:T(128)S(1)} %reshape.118.blocks_ref, f32[3,16,32,128]{3,2,1,0:T(8,128)S(1)} %pack.43.refs_2_.refs_0_, f32[3,16,32,128]{3,2,1,0:T(8,128)S(1)} %collective-permute-done.50.refs_0_.refs_1_, ...), custom_call_target="tpu_custom_call", output_to_operand_aliasing={{0}: (9, {})} | custom-call | flops 1207959552 | bytes 10485760 | tf_op jit(solution)/shard_map/correlate/pallas_call | solution.py:457
  (225 shorter events, 124.5 us)
Async XLA Ops:
  38.1 23.2 %collective-permute-start.33 = (f32[16,32,128]{2,1,0:T(8,128)}, f32[16,32,128]{2,1,0:T(8,128)}, u32[]{:S(2)}, u32[]{:S(2)}) collective-permute-start(f32[16,32,128]{2,1,0:T(8,128)} %get-tuple-element.152), channel_id=1, source_target_pairs={{0,24},{4,28},{8,16},{12,20},{16,8},{20,12},{24,0},{28,4},{1,25},{... | collective-permute-start | bytes 786440 | tf_op jit(solution)/shard_map/ppermute | solution.py:29
  40.9 20.4 %collective-permute-start.34 = (f32[16,32,128]{2,1,0:T(8,128)}, f32[16,32,128]{2,1,0:T(8,128)}, u32[]{:S(2)}, u32[]{:S(2)}) collective-permute-start(f32[16,32,128]{2,1,0:T(8,128)} %get-tuple-element.153), channel_id=1, source_target_pairs={{0,8},{4,12},{8,0},{12,4},{16,24},{20,28},{24,16},{28,20},{1,9},{5... | collective-permute-start | bytes 786440 | tf_op jit(solution)/shard_map/ppermute | solution.py:29
  62.7 27.1 %collective-permute-start.37 = (f32[4,16,32,128]{3,2,1,0:T(8,128)S(1)}, f32[4,16,32,128]{3,2,1,0:T(8,128)S(1)}, u32[]{:S(2)}, u32[]{:S(2)}) collective-permute-start(f32[4,16,32,128]{3,2,1,0:T(8,128)S(1)} %pack.30.refs_0_.refs_3_), channel_id=1, source_target_pairs={{0,2},{1,3},{2,0},{3,1},{4,6},{5,7},{6,4},{7,5},{8,10},{9,11},{10,... | collective-permute-start | bytes 3145736 | tf_op jit(solution)/shard_map/ppermute | solution.py:29
  64.7 25.1 %collective-permute-start.30 = (f32[16,32,128]{2,1,0:T(8,128)S(1)}, f32[16,32,128]{2,1,0:T(8,128)S(1)}, u32[]{:S(2)}, u32[]{:S(2)}) collective-permute-start(f32[16,32,128]{2,1,0:T(8,128)S(1)} %get-tuple-element.149), channel_id=1, source_target_pairs={{0,24},{4,28},{8,16},{12,20},{16,8},{20,12},{24,0},{28,4},{1,25},{... | collective-permute-start | bytes 786440 | tf_op jit(solution)/shard_map/ppermute | solution.py:29
  66.2 23.6 %collective-permute-start.31 = (f32[16,32,128]{2,1,0:T(8,128)S(1)}, f32[16,32,128]{2,1,0:T(8,128)S(1)}, u32[]{:S(2)}, u32[]{:S(2)}) collective-permute-start(f32[16,32,128]{2,1,0:T(8,128)S(1)} %get-tuple-element.150), channel_id=1, source_target_pairs={{0,8},{4,12},{8,0},{12,4},{16,24},{20,28},{24,16},{28,20},{1,9},{5... | collective-permute-start | bytes 786440 | tf_op jit(solution)/shard_map/ppermute | solution.py:29
  93.5 26.6 %collective-permute-start.38 = (f32[4,16,32,128]{3,2,1,0:T(8,128)S(1)}, f32[4,16,32,128]{3,2,1,0:T(8,128)S(1)}, u32[]{:S(2)}, u32[]{:S(2)}) collective-permute-start(f32[4,16,32,128]{3,2,1,0:T(8,128)S(1)} %pack.31.refs_2_.refs_0_.refs_3_), channel_id=1, source_target_pairs={{0,2},{1,3},{2,0},{3,1},{4,6},{5,7},{6,4},{7,5},{8,10},{9,11},{10,... | collective-permute-start | bytes 3145736 | tf_op jit(solution)/shard_map/ppermute | solution.py:29
  95.0 25.1 %collective-permute-start.26 = (f32[16,32,128]{2,1,0:T(8,128)}, f32[16,32,128]{2,1,0:T(8,128)}, u32[]{:S(2)}, u32[]{:S(2)}) collective-permute-start(f32[16,32,128]{2,1,0:T(8,128)} %get-tuple-element.142), channel_id=1, source_target_pairs={{0,24},{4,28},{8,16},{12,20},{16,8},{20,12},{24,0},{28,4},{1,25},{... | collective-permute-start | bytes 786440 | tf_op jit(solution)/shard_map/ppermute | solution.py:29
  96.4 23.7 %collective-permute-start.27 = (f32[16,32,128]{2,1,0:T(8,128)}, f32[16,32,128]{2,1,0:T(8,128)}, u32[]{:S(2)}, u32[]{:S(2)}) collective-permute-start(f32[16,32,128]{2,1,0:T(8,128)} %get-tuple-element.143), channel_id=1, source_target_pairs={{0,8},{4,12},{8,0},{12,4},{16,24},{20,28},{24,16},{28,20},{1,9},{5... | collective-permute-start | bytes 786440 | tf_op jit(solution)/shard_map/ppermute | solution.py:29
  101.2 20.3 %collective-permute-start.11 = (f32[4,2,8,16,128]{4,3,2,1,0:T(8,128)}, f32[4,2,8,16,128]{4,3,2,1,0:T(8,128)}, u32[]{:S(2)}, u32[]{:S(2)}) collective-permute-start(f32[4,2,8,16,128]{4,3,2,1,0:T(8,128)} %copy-done.38), channel_id=1, source_target_pairs={{0,4},{4,0},{8,12},{12,8},{16,20},{20,16},{24,28},{28,24},{1,5},{5... | collective-permute-start | bytes 1572872 | tf_op jit(solution)/shard_map/ppermute | solution.py:29
  122.8 24.7 %collective-permute-start.40 = (f32[4,16,32,128]{3,2,1,0:T(8,128)S(1)}, f32[4,16,32,128]{3,2,1,0:T(8,128)S(1)}, u32[]{:S(2)}, u32[]{:S(2)}) collective-permute-start(f32[4,16,32,128]{3,2,1,0:T(8,128)S(1)} %pack.33.refs_2_.refs_0_.refs_3_), channel_id=1, source_target_pairs={{0,2},{1,3},{2,0},{3,1},{4,6},{5,7},{6,4},{7,5},{8,10},{9,11},{10,... | collective-permute-start | bytes 3145736 | tf_op jit(solution)/shard_map/ppermute | solution.py:29
  122.9 24.3 %collective-permute-start.23 = (f32[16,32,128]{2,1,0:T(8,128)S(1)}, f32[16,32,128]{2,1,0:T(8,128)S(1)}, u32[]{:S(2)}, u32[]{:S(2)}) collective-permute-start(f32[16,32,128]{2,1,0:T(8,128)S(1)} %copy-done.40), channel_id=1, source_target_pairs={{0,24},{4,28},{8,16},{12,20},{16,8},{20,12},{24,0},{28,4},{1,25},{... | collective-permute-start | bytes 786440 | tf_op jit(solution)/shard_map/ppermute | solution.py:29
  123.9 23.3 %collective-permute-start.24 = (f32[16,32,128]{2,1,0:T(8,128)S(1)}, f32[16,32,128]{2,1,0:T(8,128)S(1)}, u32[]{:S(2)}, u32[]{:S(2)}) collective-permute-start(f32[16,32,128]{2,1,0:T(8,128)S(1)} %get-tuple-element.139), channel_id=1, source_target_pairs={{0,8},{4,12},{8,0},{12,4},{16,24},{20,28},{24,16},{28,20},{1,9},{5... | collective-permute-start | bytes 786440 | tf_op jit(solution)/shard_map/ppermute | solution.py:29
  149.3 24.5 %collective-permute-start.42 = (f32[4,16,32,128]{3,2,1,0:T(8,128)S(1)}, f32[4,16,32,128]{3,2,1,0:T(8,128)S(1)}, u32[]{:S(2)}, u32[]{:S(2)}) collective-permute-start(f32[4,16,32,128]{3,2,1,0:T(8,128)S(1)} %pack.35.refs_2_.refs_0_.refs_3_), channel_id=1, source_target_pairs={{0,2},{1,3},{2,0},{3,1},{4,6},{5,7},{6,4},{7,5},{8,10},{9,11},{10,... | collective-permute-start | bytes 3145736 | tf_op jit(solution)/shard_map/ppermute | solution.py:29
  149.5 24.4 %collective-permute-start.20 = (f32[16,32,128]{2,1,0:T(8,128)S(1)}, f32[16,32,128]{2,1,0:T(8,128)S(1)}, u32[]{:S(2)}, u32[]{:S(2)}) collective-permute-start(f32[16,32,128]{2,1,0:T(8,128)S(1)} %get-tuple-element.133), channel_id=1, source_target_pairs={{0,24},{4,28},{8,16},{12,20},{16,8},{20,12},{24,0},{28,4},{1,25},{... | collective-permute-start | bytes 786440 | tf_op jit(solution)/shard_map/ppermute | solution.py:29
  150.9 23.0 %collective-permute-start.21 = (f32[16,32,128]{2,1,0:T(8,128)S(1)}, f32[16,32,128]{2,1,0:T(8,128)S(1)}, u32[]{:S(2)}, u32[]{:S(2)}) collective-permute-start(f32[16,32,128]{2,1,0:T(8,128)S(1)} %get-tuple-element.134), channel_id=1, source_target_pairs={{0,8},{4,12},{8,0},{12,4},{16,24},{20,28},{24,16},{28,20},{1,9},{5... | collective-permute-start | bytes 786440 | tf_op jit(solution)/shard_map/ppermute | solution.py:29
  177.1 24.8 %collective-permute-start.44 = (f32[4,16,32,128]{3,2,1,0:T(8,128)S(1)}, f32[4,16,32,128]{3,2,1,0:T(8,128)S(1)}, u32[]{:S(2)}, u32[]{:S(2)}) collective-permute-start(f32[4,16,32,128]{3,2,1,0:T(8,128)S(1)} %pack.37.refs_2_.refs_0_.refs_3_), channel_id=1, source_target_pairs={{0,2},{1,3},{2,0},{3,1},{4,6},{5,7},{6,4},{7,5},{8,10},{9,11},{10,... | collective-permute-start | bytes 3145736 | tf_op jit(solution)/shard_map/ppermute | solution.py:29
  177.1 24.7 %collective-permute-start.13 = (f32[16,32,128]{2,1,0:T(8,128)S(1)}, f32[16,32,128]{2,1,0:T(8,128)S(1)}, u32[]{:S(2)}, u32[]{:S(2)}) collective-permute-start(f32[16,32,128]{2,1,0:T(8,128)S(1)} %get-tuple-element.124), channel_id=1, source_target_pairs={{0,24},{4,28},{8,16},{12,20},{16,8},{20,12},{24,0},{28,4},{1,25},{... | collective-permute-start | bytes 786440 | tf_op jit(solution)/shard_map/ppermute | solution.py:29
  178.5 23.3 %collective-permute-start.14 = (f32[16,32,128]{2,1,0:T(8,128)S(1)}, f32[16,32,128]{2,1,0:T(8,128)S(1)}, u32[]{:S(2)}, u32[]{:S(2)}) collective-permute-start(f32[16,32,128]{2,1,0:T(8,128)S(1)} %get-tuple-element.125), channel_id=1, source_target_pairs={{0,8},{4,12},{8,0},{12,4},{16,24},{20,28},{24,16},{28,20},{1,9},{5... | collective-permute-start | bytes 786440 | tf_op jit(solution)/shard_map/ppermute | solution.py:29
  204.5 24.8 %collective-permute-start.46 = (f32[4,16,32,128]{3,2,1,0:T(8,128)S(1)}, f32[4,16,32,128]{3,2,1,0:T(8,128)S(1)}, u32[]{:S(2)}, u32[]{:S(2)}) collective-permute-start(f32[4,16,32,128]{3,2,1,0:T(8,128)S(1)} %pack.39.refs_2_.refs_0_.refs_3_), channel_id=1, source_target_pairs={{0,2},{1,3},{2,0},{3,1},{4,6},{5,7},{6,4},{7,5},{8,10},{9,11},{10,... | collective-permute-start | bytes 3145736 | tf_op jit(solution)/shard_map/ppermute | solution.py:29
  207.1 22.1 %collective-permute-start.9 = (f32[16,32,128]{2,1,0:T(8,128)S(1)}, f32[16,32,128]{2,1,0:T(8,128)S(1)}, u32[]{:S(2)}, u32[]{:S(2)}) collective-permute-start(f32[16,32,128]{2,1,0:T(8,128)S(1)} %get-tuple-element.116), channel_id=1, source_target_pairs={{0,24},{4,28},{8,16},{12,20},{16,8},{20,12},{24,0},{28,4},{1,25},{... | collective-permute-start | bytes 786440 | tf_op jit(solution)/shard_map/ppermute | solution.py:29
  230.9 24.8 %collective-permute-start.48 = (f32[4,16,32,128]{3,2,1,0:T(8,128)S(1)}, f32[4,16,32,128]{3,2,1,0:T(8,128)S(1)}, u32[]{:S(2)}, u32[]{:S(2)}) collective-permute-start(f32[4,16,32,128]{3,2,1,0:T(8,128)S(1)} %pack.41.refs_2_.refs_0_.refs_4_), channel_id=1, source_target_pairs={{0,2},{1,3},{2,0},{3,1},{4,6},{5,7},{6,4},{7,5},{8,10},{9,11},{10,... | collective-permute-start | bytes 3145736 | tf_op jit(solution)/shard_map/ppermute | solution.py:29
  230.9 24.8 %collective-permute-start.5 = (f32[16,32,128]{2,1,0:T(8,128)S(1)}, f32[16,32,128]{2,1,0:T(8,128)S(1)}, u32[]{:S(2)}, u32[]{:S(2)}) collective-permute-start(f32[16,32,128]{2,1,0:T(8,128)S(1)} %get-tuple-element.111), channel_id=1, source_target_pairs={{0,24},{4,28},{8,16},{12,20},{16,8},{20,12},{24,0},{28,4},{1,25},{... | collective-permute-start | bytes 786440 | tf_op jit(solution)/shard_map/ppermute | solution.py:29
  232.4 23.3 %collective-permute-start.6 = (f32[16,32,128]{2,1,0:T(8,128)S(1)}, f32[16,32,128]{2,1,0:T(8,128)S(1)}, u32[]{:S(2)}, u32[]{:S(2)}) collective-permute-start(f32[16,32,128]{2,1,0:T(8,128)S(1)} %get-tuple-element.112), channel_id=1, source_target_pairs={{0,8},{4,12},{8,0},{12,4},{16,24},{20,28},{24,16},{28,20},{1,9},{5... | collective-permute-start | bytes 786440 | tf_op jit(solution)/shard_map/ppermute | solution.py:29
  257.2 20.3 %collective-permute-start.51 = (f32[3,16,32,128]{3,2,1,0:T(8,128)S(1)}, f32[3,16,32,128]{3,2,1,0:T(8,128)S(1)}, u32[]{:S(2)}, u32[]{:S(2)}) collective-permute-start(f32[3,16,32,128]{3,2,1,0:T(8,128)S(1)} %pack.43.refs_2_.refs_0_), channel_id=1, source_target_pairs={{0,1},{1,0},{2,3},{3,2},{4,5},{5,4},{6,7},{7,6},{8,9},{9,8},{10,11... | collective-permute-start | bytes 2359304 | tf_op jit(solution)/shard_map/ppermute | solution.py:29
  (76 other events, 693.9 us)
where the time goes:
time: 286 us; the launch traced here: 285 us
  waiting for transfers between devices  131 us (46%)
  Pallas kernels  87.7 us (31%)
  starting transfers between devices  52.4 us (18%)
  local copies, waits for them, and re-layouts  13.3 us (5%)
    ppermute x53, waiting for transfers between devices, swapped(): lax.ppermute(value, axis, [(source, source ^ mask) for source in range(co...  131 us
    ppermute x53, starting transfers between devices, swapped(): lax.ppermute(value, axis, [(source, source ^ mask) for source in range(co...  49.7 us
    pallas_call x8, Pallas kernels, correlated(): pl.pallas_call(functools.partial(correlate_kernel, slots, tiles, order),...  44.6 us
    pallas_call x23, Pallas kernels, packed(): pl.pallas_call(functools.partial(pack_kernel, counts), grid=(values[0].sh...  14.2 us
    pallas_call x5, Pallas kernels, transformed(): pl.pallas_call(functools.partial(transform_kernel, groups, pieces), grid=...  11.7 us
    unnamed x93, local copies, waits for them, and re-layouts  11.7 us
    pallas_call x8, Pallas kernels, merged(): pl.pallas_call(functools.partial(merge_kernel, count, groups, piece), in_...  11.4 us
    pallas_call x2, Pallas kernels, filtered_samples(): pl.pallas_call(functools.partial(filter_kernel, count), grid=(inputs // w...  5.88 us
  transfers between devices with their start and end apart: 54, of which 25 were waited for; matrix products, arithmetic and copies ran while one was open for 0% of the time, Pallas kernels for 26%

commit v1 on v0

--- a/solution.py
+++ b/solution.py
@@ -433,7 +433,7 @@
             out_ref[slot, channel, 1] = value[:, BLOCK:]
 
 
-def correlated(order, tile_slot, tile_blocks, units, before, visibility, residue, first, total, slots):
+def correlated(order, tile_slot, tile_blocks, units, before, visibility, residue, first, total, slots, at):
     tiles = sum(1 if unit.ndim == 4 else unit.shape[0] for unit in units)
     blocks = len(order)
     piece, depth, lanes = units[0].shape[-3:]
@@ -448,7 +448,7 @@
         )
 
     in_specs = [spec(unit, blocks - 1, 0) for unit in units]
-    in_specs += [spec(unit, 1, unit.shape[-4] - 1) for unit in before]
+    in_specs += [spec(unit, 1, at % unit.shape[-4]) for unit in before]
     aliases = {}
     if visibility is not None:
         operands.append(visibility)
@@ -548,13 +548,10 @@
     def products(piece, arrays, before, visibility):
         return correlated(
             order, tile_slot, tile_blocks, arrays, before, visibility,
-            piece // halves, piece % halves * size, channels // RADIX, slots,
+            piece // halves, piece % halves * size, channels // RADIX, slots, blocks - 1 if piece == 0 else -1,
         )
 
-    (seed,) = packed([list(units[0][-1:])], [])
-    seed_across = swapped(seed, "tile", 2)
-    (both,) = packed([[seed, seed_across]], [])
-    before = [seed, seed_across, swapped(both, "tile", 1)]
+    before = None
     visibility = None
     finished = []
     pair = None
@@ -567,10 +564,9 @@
                 after.append(units[later][0])
         else:
             after = [units[1][0], away[2][0]] + [near[residue * halves][0] for residue in range(2, RADIX)]
-            after += before[2:]
         after += finished[piece - 2 : piece - 1] if piece >= 2 else []
         following = list(units[piece + 1][-1:]) if piece + 1 < count else []
-        (own,) = packed([turned[:-1] + following], after, LONG)
+        (own,) = packed([turned[: None if piece == 0 else -1] + following], after, LONG)
         if piece + 1 < count:
             turned = along(piece + 1)
         across = swapped(own, "tile", 2)
@@ -579,7 +575,7 @@
         if pair:
             (both,) = packed([pair], [own] + (away[piece + 3][-1:] if piece + 3 < count else []))
             arrays = pair + [swapped(both, "tile", 1)]
-            visibility, token = products(piece - 1, arrays, before, visibility)
+            visibility, token = products(piece - 1, arrays, before or arrays, visibility)
             finished.append(token)
             before = arrays
         pair = [own, across]

time: 286 us -> 287 us (level)
    ppermute x53 -> x51, waiting for transfers between devices: 131 us -> 132 us  [swapped(): lax.ppermute(value, axis, [(source, source ^ mask) for source in range(co...]
    unnamed x93 -> x95, local copies, waits for them, and re-layouts: 11.7 us -> 12.1 us
    ppermute x53 -> x51, starting transfers between devices: 49.7 us -> 49.4 us  [swapped(): lax.ppermute(value, axis, [(source, source ^ mask) for source in range(co...]
    pallas_call x23 -> x21, Pallas kernels: 14.2 us -> 14.2 us  [packed(): pl.pallas_call(functools.partial(pack_kernel, counts), grid=(values[0].sh...]
  transfers between devices with their start and end apart: 54 -> 52, of which waited for: 25 -> 24; matrix products, arithmetic and copies ran while one was open for 0% -> 0% of each run, Pallas kernels for 26% -> 26%
where the time goes in v1:
time: 287 us; the launch traced here: 286 us
  waiting for transfers between devices  132 us (46%)
  Pallas kernels  87.3 us (30%)
  starting transfers between devices  52.1 us (18%)
  local copies, waits for them, and re-layouts  13.7 us (5%)
    ppermute x51, waiting for transfers between devices, swapped(): lax.ppermute(value, axis, [(source, source ^ mask) for source in range(co...  132 us
    ppermute x51, starting transfers between devices, swapped(): lax.ppermute(value, axis, [(source, source ^ mask) for source in range(co...  49.4 us
    pallas_call x8, Pallas kernels, correlated(): pl.pallas_call(functools.partial(correlate_kernel, slots, tiles, order),...  44.3 us
    pallas_call x21, Pallas kernels, packed(): pl.pallas_call(functools.partial(pack_kernel, counts), grid=(values[0].sh...  14.2 us
    unnamed x95, local copies, waits for them, and re-layouts  12.1 us
    pallas_call x5, Pallas kernels, transformed(): pl.pallas_call(functools.partial(transform_kernel, groups, pieces), grid=...  11.7 us
    pallas_call x8, Pallas kernels, merged(): pl.pallas_call(functools.partial(merge_kernel, count, groups, piece), in_...  11.2 us
    pallas_call x2, Pallas kernels, filtered_samples(): pl.pallas_call(functools.partial(filter_kernel, count), grid=(inputs // w...  5.88 us
  transfers between devices with their start and end apart: 52, of which 24 were waited for; matrix products, arithmetic and copies ran while one was open for 0% of the time, Pallas kernels for 26%

profile of v1, /device:TPU:13, one launch (start us, length us, event | category | flops | bytes accessed | tf_op | source)
XLA Modules:
  0.0 286.1 jit_solution(10356979576552325112)
XLA Ops:
  7.7 4.3 %filter.2 = (bf16[16,64,512]{2,1,0:T(8,128)(2,1)S(1)}, bf16[16,64,512]{2,1,0:T(8,128)(2,1)S(1)}, bf16[16,64,512]{2,1,0:T(8,128)(2,1)S(1)}, bf16[16,64,512]{2,1,0...) custom-call(f32[2,16,64,1024]{3,2,1,0:T(8,128)S(1)} %copy-done, ...), custom_call_target="tpu_custom_call" | custom-call | flops 25165824 | bytes 12582912 | tf_op jit(solution)/shard_map/filter/pallas_call | solution.py:196
  20.7 5.7 %collective-permute-done.2.refs_1_ = f32[4,2,2,16,128]{4,3,2,1,0:T(8,128)S(1)} collective-permute-done((f32[4,2,2,16,128]{4,3,2,1,0:T(8,128)S(1)}, f32[4,2,2,16,128]{4,3,2,1,0:T(8,128)S(1)}, u32[]{:S(2)}, u32[]{:S(2)}) %collective-permute-start.2) | collective-permute-done | bytes 131104 | tf_op jit(solution)/shard_map/ppermute | solution.py:29
  44.2 6.2 %collective-permute-done.32.refs_0_ = f32[16,32,128]{2,1,0:T(8,128)} collective-permute-done((f32[16,32,128]{2,1,0:T(8,128)}, f32[16,32,128]{2,1,0:T(8,128)}, u32[]{:S(2)}, u32[]{:S(2)}) %collective-permute-start.32) | collective-permute-done | bytes 262176 | tf_op jit(solution)/shard_map/ppermute | solution.py:29
  50.4 5.6 %collective-permute-done.33.refs_1_ = f32[16,32,128]{2,1,0:T(8,128)} collective-permute-done((f32[16,32,128]{2,1,0:T(8,128)}, f32[16,32,128]{2,1,0:T(8,128)}, u32[]{:S(2)}, u32[]{:S(2)}) %collective-permute-start.33) | collective-permute-done | bytes 262176 | tf_op jit(solution)/shard_map/ppermute | solution.py:29
  66.3 6.0 %collective-permute-done.17.refs_1_ = f32[4,2,8,16,128]{4,3,2,1,0:T(8,128)S(1)} collective-permute-done((f32[4,2,8,16,128]{4,3,2,1,0:T(8,128)S(1)}, f32[4,2,8,16,128]{4,3,2,1,0:T(8,128)S(1)}, u32[]{:S(2)}, u32[]{:S(2)}) %collective-permute-start.17) | collective-permute-done | bytes 524320 | tf_op jit(solution)/shard_map/ppermute | solution.py:29
  76.6 9.5 %collective-permute-done.30.refs_1_ = f32[16,32,128]{2,1,0:T(8,128)S(1)} collective-permute-done((f32[16,32,128]{2,1,0:T(8,128)S(1)}, f32[16,32,128]{2,1,0:T(8,128)S(1)}, u32[]{:S(2)}, u32[]{:S(2)}) %collective-permute-start.30) | collective-permute-done | bytes 262176 | tf_op jit(solution)/shard_map/ppermute | solution.py:29
  104.5 5.3 %correlate.8 = (f32[3,32,4,2,128,128]{5,4,3,2,1,0:T(8,128)}, f32[8,128]{1,0:T(8,128)S(1)}) custom-call(s32[10]{0:T(128)S(1)} %copy-done.38, s32[20]{0:T(128)S(1)} %reshape.118.blocks_ref, f32[5,16,32,128]{3,2,1,0:T(8,128)S(1)} %copy-done.4, f32[5,16,32,128]{3,2,1,0:T(8,128)S(1)} %copy-done.7, ...), custom_call_target="tpu_custom_call" | custom-call | flops 1207959552 | bytes 10485760 | tf_op jit(solution)/shard_map/correlate/pallas_call | solution.py:457
  111.7 8.5 %collective-permute-done.26.refs_1_ = f32[16,32,128]{2,1,0:T(8,128)} collective-permute-done((f32[16,32,128]{2,1,0:T(8,128)}, f32[16,32,128]{2,1,0:T(8,128)}, u32[]{:S(2)}, u32[]{:S(2)}) %collective-permute-start.26) | collective-permute-done | bytes 262176 | tf_op jit(solution)/shard_map/ppermute | solution.py:29
  130.6 6.5 %correlate.9 = (f32[3,32,4,2,128,128]{5,4,3,2,1,0:T(8,128)}, f32[8,128]{1,0:T(8,128)S(1)}) custom-call(s32[10]{0:T(128)S(1)} %copy-done.38, s32[20]{0:T(128)S(1)} %reshape.118.blocks_ref, f32[4,16,32,128]{3,2,1,0:T(8,128)} %pack.27.refs_2_.refs_0_.refs_3_, ...), custom_call_target="tpu_custom_call", output_to_operand_aliasing={{0}: (8, {})} | custom-call | flops 1207959552 | bytes 10485760 | tf_op jit(solution)/shard_map/correlate/pallas_call | solution.py:457
  141.2 7.7 %collective-permute-done.23.refs_1_ = f32[16,32,128]{2,1,0:T(8,128)S(1)} collective-permute-done((f32[16,32,128]{2,1,0:T(8,128)S(1)}, f32[16,32,128]{2,1,0:T(8,128)S(1)}, u32[]{:S(2)}, u32[]{:S(2)}) %collective-permute-start.23) | collective-permute-done | bytes 262176 | tf_op jit(solution)/shard_map/ppermute | solution.py:29
  157.1 6.2 %correlate.10 = (f32[3,32,4,2,128,128]{5,4,3,2,1,0:T(8,128)}, f32[8,128]{1,0:T(8,128)S(1)}) custom-call(s32[10]{0:T(128)S(1)} %copy-done.38, s32[20]{0:T(128)S(1)} %reshape.118.blocks_ref, f32[4,16,32,128]{3,2,1,0:T(8,128)S(1)} %pack.29.refs_2_.refs_0_.refs_3_, ...), custom_call_target="tpu_custom_call", output_to_operand_aliasing={{0}: (8, {})} | custom-call | flops 1207959552 | bytes 10485760 | tf_op jit(solution)/shard_map/correlate/pallas_call | solution.py:457
  167.3 7.9 %collective-permute-done.20.refs_1_ = f32[16,32,128]{2,1,0:T(8,128)S(1)} collective-permute-done((f32[16,32,128]{2,1,0:T(8,128)S(1)}, f32[16,32,128]{2,1,0:T(8,128)S(1)}, u32[]{:S(2)}, u32[]{:S(2)}) %collective-permute-start.20) | collective-permute-done | bytes 262176 | tf_op jit(solution)/shard_map/ppermute | solution.py:29
  183.6 5.3 %correlate.11 = (f32[3,32,4,2,128,128]{5,4,3,2,1,0:T(8,128)}, f32[8,128]{1,0:T(8,128)S(1)}) custom-call(s32[10]{0:T(128)S(1)} %copy-done.38, s32[20]{0:T(128)S(1)} %reshape.118.blocks_ref, f32[4,16,32,128]{3,2,1,0:T(8,128)S(1)} %copy-done.13, f32[4,16,32,128]{3,2,1,0:T(8,128)S(1)} %collective-permute-done.40.refs_4_.refs_1_, ...), custom_call_target="tpu_custom_call", output_to_operand_aliasing={{0}: (8, {})} | custom-call | flops 1207959552 | bytes 10485760 | tf_op jit(solution)/shard_map/correlate/pallas_call | solution.py:457
  188.9 6.6 %collective-permute-done.12.refs_0_ = f32[16,32,128]{2,1,0:T(8,128)S(1)} collective-permute-done((f32[16,32,128]{2,1,0:T(8,128)S(1)}, f32[16,32,128]{2,1,0:T(8,128)S(1)}, u32[]{:S(2)}, u32[]{:S(2)}) %collective-permute-start.12) | collective-permute-done | bytes 262176 | tf_op jit(solution)/shard_map/ppermute | solution.py:29
  195.5 7.8 %collective-permute-done.13.refs_1_ = f32[16,32,128]{2,1,0:T(8,128)S(1)} collective-permute-done((f32[16,32,128]{2,1,0:T(8,128)S(1)}, f32[16,32,128]{2,1,0:T(8,128)S(1)}, u32[]{:S(2)}, u32[]{:S(2)}) %collective-permute-start.13) | collective-permute-done | bytes 262176 | tf_op jit(solution)/shard_map/ppermute | solution.py:29
  209.7 5.3 %correlate.12 = (f32[3,32,4,2,128,128]{5,4,3,2,1,0:T(8,128)}, f32[8,128]{1,0:T(8,128)S(1)}) custom-call(s32[10]{0:T(128)S(1)} %copy-done.38, s32[20]{0:T(128)S(1)} %reshape.118.blocks_ref, f32[4,16,32,128]{3,2,1,0:T(8,128)S(1)} %copy-done.10, f32[4,16,32,128]{3,2,1,0:T(8,128)S(1)} %collective-permute-done.42.refs_4_.refs_1_, ...), custom_call_target="tpu_custom_call", output_to_operand_aliasing={{0}: (8, {})} | custom-call | flops 1207959552 | bytes 10485760 | tf_op jit(solution)/shard_map/correlate/pallas_call | solution.py:457
  215.0 5.4 %collective-permute-done.10.refs_2_ = f32[16,32,128]{2,1,0:T(8,128)S(1)} collective-permute-done((f32[16,32,128]{2,1,0:T(8,128)S(1)}, f32[16,32,128]{2,1,0:T(8,128)S(1)}, u32[]{:S(2)}, u32[]{:S(2)}) %collective-permute-start.10) | collective-permute-done | bytes 262176 | tf_op jit(solution)/shard_map/ppermute | solution.py:29
  220.4 10.4 %collective-permute-done.9.refs_1_ = f32[16,32,128]{2,1,0:T(8,128)S(1)} collective-permute-done((f32[16,32,128]{2,1,0:T(8,128)S(1)}, f32[16,32,128]{2,1,0:T(8,128)S(1)}, u32[]{:S(2)}, u32[]{:S(2)}) %collective-permute-start.9) | collective-permute-done | bytes 262176 | tf_op jit(solution)/shard_map/ppermute | solution.py:29
  236.1 5.3 %correlate.13 = (f32[3,32,4,2,128,128]{5,4,3,2,1,0:T(8,128)}, f32[8,128]{1,0:T(8,128)S(1)}) custom-call(s32[10]{0:T(128)S(1)} %copy-done.38, s32[20]{0:T(128)S(1)} %reshape.118.blocks_ref, f32[4,16,32,128]{3,2,1,0:T(8,128)S(1)} %pack.35.refs_2_.refs_0_.refs_3_, ...), custom_call_target="tpu_custom_call", output_to_operand_aliasing={{0}: (8, {})} | custom-call | flops 1207959552 | bytes 10485760 | tf_op jit(solution)/shard_map/correlate/pallas_call | solution.py:457
  241.4 7.9 %collective-permute-done.4.refs_0_ = f32[16,32,128]{2,1,0:T(8,128)S(1)} collective-permute-done((f32[16,32,128]{2,1,0:T(8,128)S(1)}, f32[16,32,128]{2,1,0:T(8,128)S(1)}, u32[]{:S(2)}, u32[]{:S(2)}) %collective-permute-start.4) | collective-permute-done | bytes 262176 | tf_op jit(solution)/shard_map/ppermute | solution.py:29
  249.3 7.8 %collective-permute-done.5.refs_1_ = f32[16,32,128]{2,1,0:T(8,128)S(1)} collective-permute-done((f32[16,32,128]{2,1,0:T(8,128)S(1)}, f32[16,32,128]{2,1,0:T(8,128)S(1)}, u32[]{:S(2)}, u32[]{:S(2)}) %collective-permute-start.5) | collective-permute-done | bytes 262176 | tf_op jit(solution)/shard_map/ppermute | solution.py:29
  262.4 5.3 %correlate.14 = (f32[3,32,4,2,128,128]{5,4,3,2,1,0:T(8,128)}, f32[8,128]{1,0:T(8,128)S(1)}) custom-call(s32[10]{0:T(128)S(1)} %copy-done.38, s32[20]{0:T(128)S(1)} %reshape.118.blocks_ref, f32[4,16,32,128]{3,2,1,0:T(8,128)S(1)} %pack.37.refs_2_.refs_0_.refs_4_, ...), custom_call_target="tpu_custom_call", output_to_operand_aliasing={{0}: (8, {})} | custom-call | flops 1207959552 | bytes 10485760 | tf_op jit(solution)/shard_map/correlate/pallas_call | solution.py:457
  267.7 10.1 %collective-permute-done.48.refs_0_.refs_1_ = f32[3,16,32,128]{3,2,1,0:T(8,128)S(1)} collective-permute-done((f32[3,16,32,128]{3,2,1,0:T(8,128)S(1)}, f32[3,16,32,128]{3,2,1,0:T(8,128)S(1)}, u32[]{:S(2)}, u32[]{:S(2)}) %collective-permute-start.48) | collective-permute-done | bytes 786464 | tf_op jit(solution)/shard_map/ppermute | solution.py:29
  280.8 5.3 %correlate.15 = (f32[3,32,4,2,128,128]{5,4,3,2,1,0:T(8,128)}, f32[8,128]{1,0:T(8,128)}) custom-call(s32[10]{0:T(128)S(1)} %copy-done.38, s32[20]{0:T(128)S(1)} %reshape.118.blocks_ref, f32[3,16,32,128]{3,2,1,0:T(8,128)S(1)} %pack.39.refs_2_.refs_0_, f32[3,16,32,128]{3,2,1,0:T(8,128)S(1)} %collective-permute-done.48.refs_0_.refs_1_, ...), custom_call_target="tpu_custom_call", output_to_operand_aliasing={{0}: (9, {})} | custom-call | flops 1207959552 | bytes 10485760 | tf_op jit(solution)/shard_map/correlate/pallas_call | solution.py:457
  (221 shorter events, 123.8 us)
Async XLA Ops:
  32.9 23.1 %collective-permute-start.33 = (f32[16,32,128]{2,1,0:T(8,128)}, f32[16,32,128]{2,1,0:T(8,128)}, u32[]{:S(2)}, u32[]{:S(2)}) collective-permute-start(f32[16,32,128]{2,1,0:T(8,128)} %get-tuple-element.152), channel_id=1, source_target_pairs={{0,24},{4,28},{8,16},{12,20},{16,8},{20,12},{24,0},{28,4},{1,25},{... | collective-permute-start | bytes 786440 | tf_op jit(solution)/shard_map/ppermute | solution.py:29
  32.9 23.1 %collective-permute-start.34 = (f32[16,32,128]{2,1,0:T(8,128)}, f32[16,32,128]{2,1,0:T(8,128)}, u32[]{:S(2)}, u32[]{:S(2)}) collective-permute-start(f32[16,32,128]{2,1,0:T(8,128)} %get-tuple-element.153), channel_id=1, source_target_pairs={{0,8},{4,12},{8,0},{12,4},{16,24},{20,28},{24,16},{28,20},{1,9},{5... | collective-permute-start | bytes 786440 | tf_op jit(solution)/shard_map/ppermute | solution.py:29
  57.4 30.6 %collective-permute-start.35 = (f32[5,16,32,128]{3,2,1,0:T(8,128)S(1)}, f32[5,16,32,128]{3,2,1,0:T(8,128)S(1)}, u32[]{:S(2)}, u32[]{:S(2)}) collective-permute-start(f32[5,16,32,128]{3,2,1,0:T(8,128)S(1)} %pack.26.refs_0_.refs_3_), channel_id=1, source_target_pairs={{0,2},{1,3},{2,0},{3,1},{4,6},{5,7},{6,4},{7,5},{8,10},{9,11},{10,... | collective-permute-start | bytes 3932168 | tf_op jit(solution)/shard_map/ppermute | solution.py:29
  60.6 25.6 %collective-permute-start.30 = (f32[16,32,128]{2,1,0:T(8,128)S(1)}, f32[16,32,128]{2,1,0:T(8,128)S(1)}, u32[]{:S(2)}, u32[]{:S(2)}) collective-permute-start(f32[16,32,128]{2,1,0:T(8,128)S(1)} %get-tuple-element.149), channel_id=1, source_target_pairs={{0,24},{4,28},{8,16},{12,20},{16,8},{20,12},{24,0},{28,4},{1,25},{... | collective-permute-start | bytes 786440 | tf_op jit(solution)/shard_map/ppermute | solution.py:29
  62.7 23.5 %collective-permute-start.31 = (f32[16,32,128]{2,1,0:T(8,128)S(1)}, f32[16,32,128]{2,1,0:T(8,128)S(1)}, u32[]{:S(2)}, u32[]{:S(2)}) collective-permute-start(f32[16,32,128]{2,1,0:T(8,128)S(1)} %get-tuple-element.150), channel_id=1, source_target_pairs={{0,8},{4,12},{8,0},{12,4},{16,24},{20,28},{24,16},{28,20},{1,9},{5... | collective-permute-start | bytes 786440 | tf_op jit(solution)/shard_map/ppermute | solution.py:29
  93.0 27.3 %collective-permute-start.36 = (f32[4,16,32,128]{3,2,1,0:T(8,128)}, f32[4,16,32,128]{3,2,1,0:T(8,128)}, u32[]{:S(2)}, u32[]{:S(2)}) collective-permute-start(f32[4,16,32,128]{3,2,1,0:T(8,128)} %pack.27.refs_2_.refs_0_.refs_3_), channel_id=1, source_target_pairs={{0,2},{1,3},{2,0},{3,1},{4,6},{5,7},{6,4},{7,5},{8,10},{9,11},{10,... | collective-permute-start | bytes 3145736 | tf_op jit(solution)/shard_map/ppermute | solution.py:29
  94.4 25.9 %collective-permute-start.26 = (f32[16,32,128]{2,1,0:T(8,128)}, f32[16,32,128]{2,1,0:T(8,128)}, u32[]{:S(2)}, u32[]{:S(2)}) collective-permute-start(f32[16,32,128]{2,1,0:T(8,128)} %get-tuple-element.142), channel_id=1, source_target_pairs={{0,24},{4,28},{8,16},{12,20},{16,8},{20,12},{24,0},{28,4},{1,25},{... | collective-permute-start | bytes 786440 | tf_op jit(solution)/shard_map/ppermute | solution.py:29
  96.5 23.8 %collective-permute-start.27 = (f32[16,32,128]{2,1,0:T(8,128)}, f32[16,32,128]{2,1,0:T(8,128)}, u32[]{:S(2)}, u32[]{:S(2)}) collective-permute-start(f32[16,32,128]{2,1,0:T(8,128)} %get-tuple-element.143), channel_id=1, source_target_pairs={{0,8},{4,12},{8,0},{12,4},{16,24},{20,28},{24,16},{28,20},{1,9},{5... | collective-permute-start | bytes 786440 | tf_op jit(solution)/shard_map/ppermute | solution.py:29
  100.6 21.0 %collective-permute-start.11 = (f32[4,2,8,16,128]{4,3,2,1,0:T(8,128)}, f32[4,2,8,16,128]{4,3,2,1,0:T(8,128)}, u32[]{:S(2)}, u32[]{:S(2)}) collective-permute-start(f32[4,2,8,16,128]{4,3,2,1,0:T(8,128)} %copy-done.39), channel_id=1, source_target_pairs={{0,4},{4,0},{8,12},{12,8},{16,20},{20,16},{24,28},{28,24},{1,5},{5... | collective-permute-start | bytes 1572872 | tf_op jit(solution)/shard_map/ppermute | solution.py:29
  124.3 24.7 %collective-permute-start.38 = (f32[4,16,32,128]{3,2,1,0:T(8,128)S(1)}, f32[4,16,32,128]{3,2,1,0:T(8,128)S(1)}, u32[]{:S(2)}, u32[]{:S(2)}) collective-permute-start(f32[4,16,32,128]{3,2,1,0:T(8,128)S(1)} %pack.29.refs_2_.refs_0_.refs_3_), channel_id=1, source_target_pairs={{0,2},{1,3},{2,0},{3,1},{4,6},{5,7},{6,4},{7,5},{8,10},{9,11},{10,... | collective-permute-start | bytes 3145736 | tf_op jit(solution)/shard_map/ppermute | solution.py:29
  124.3 24.7 %collective-permute-start.23 = (f32[16,32,128]{2,1,0:T(8,128)S(1)}, f32[16,32,128]{2,1,0:T(8,128)S(1)}, u32[]{:S(2)}, u32[]{:S(2)}) collective-permute-start(f32[16,32,128]{2,1,0:T(8,128)S(1)} %copy-done.41), channel_id=1, source_target_pairs={{0,24},{4,28},{8,16},{12,20},{16,8},{20,12},{24,0},{28,4},{1,25},{... | collective-permute-start | bytes 786440 | tf_op jit(solution)/shard_map/ppermute | solution.py:29
  125.7 23.3 %collective-permute-start.24 = (f32[16,32,128]{2,1,0:T(8,128)S(1)}, f32[16,32,128]{2,1,0:T(8,128)S(1)}, u32[]{:S(2)}, u32[]{:S(2)}) collective-permute-start(f32[16,32,128]{2,1,0:T(8,128)S(1)} %get-tuple-element.139), channel_id=1, source_target_pairs={{0,8},{4,12},{8,0},{12,4},{16,24},{20,28},{24,16},{28,20},{1,9},{5... | collective-permute-start | bytes 786440 | tf_op jit(solution)/shard_map/ppermute | solution.py:29
  150.8 24.4 %collective-permute-start.40 = (f32[4,16,32,128]{3,2,1,0:T(8,128)S(1)}, f32[4,16,32,128]{3,2,1,0:T(8,128)S(1)}, u32[]{:S(2)}, u32[]{:S(2)}) collective-permute-start(f32[4,16,32,128]{3,2,1,0:T(8,128)S(1)} %pack.31.refs_2_.refs_0_.refs_3_), channel_id=1, source_target_pairs={{0,2},{1,3},{2,0},{3,1},{4,6},{5,7},{6,4},{7,5},{8,10},{9,11},{10,... | collective-permute-start | bytes 3145736 | tf_op jit(solution)/shard_map/ppermute | solution.py:29
  150.8 24.4 %collective-permute-start.20 = (f32[16,32,128]{2,1,0:T(8,128)S(1)}, f32[16,32,128]{2,1,0:T(8,128)S(1)}, u32[]{:S(2)}, u32[]{:S(2)}) collective-permute-start(f32[16,32,128]{2,1,0:T(8,128)S(1)} %get-tuple-element.133), channel_id=1, source_target_pairs={{0,24},{4,28},{8,16},{12,20},{16,8},{20,12},{24,0},{28,4},{1,25},{... | collective-permute-start | bytes 786440 | tf_op jit(solution)/shard_map/ppermute | solution.py:29
  152.4 22.9 %collective-permute-start.21 = (f32[16,32,128]{2,1,0:T(8,128)S(1)}, f32[16,32,128]{2,1,0:T(8,128)S(1)}, u32[]{:S(2)}, u32[]{:S(2)}) collective-permute-start(f32[16,32,128]{2,1,0:T(8,128)S(1)} %get-tuple-element.134), channel_id=1, source_target_pairs={{0,8},{4,12},{8,0},{12,4},{16,24},{20,28},{24,16},{28,20},{1,9},{5... | collective-permute-start | bytes 786440 | tf_op jit(solution)/shard_map/ppermute | solution.py:29
  178.5 24.8 %collective-permute-start.42 = (f32[4,16,32,128]{3,2,1,0:T(8,128)S(1)}, f32[4,16,32,128]{3,2,1,0:T(8,128)S(1)}, u32[]{:S(2)}, u32[]{:S(2)}) collective-permute-start(f32[4,16,32,128]{3,2,1,0:T(8,128)S(1)} %pack.33.refs_2_.refs_0_.refs_3_), channel_id=1, source_target_pairs={{0,2},{1,3},{2,0},{3,1},{4,6},{5,7},{6,4},{7,5},{8,10},{9,11},{10,... | collective-permute-start | bytes 3145736 | tf_op jit(solution)/shard_map/ppermute | solution.py:29
  178.6 24.7 %collective-permute-start.13 = (f32[16,32,128]{2,1,0:T(8,128)S(1)}, f32[16,32,128]{2,1,0:T(8,128)S(1)}, u32[]{:S(2)}, u32[]{:S(2)}) collective-permute-start(f32[16,32,128]{2,1,0:T(8,128)S(1)} %get-tuple-element.124), channel_id=1, source_target_pairs={{0,24},{4,28},{8,16},{12,20},{16,8},{20,12},{24,0},{28,4},{1,25},{... | collective-permute-start | bytes 786440 | tf_op jit(solution)/shard_map/ppermute | solution.py:29
  180.0 23.3 %collective-permute-start.14 = (f32[16,32,128]{2,1,0:T(8,128)S(1)}, f32[16,32,128]{2,1,0:T(8,128)S(1)}, u32[]{:S(2)}, u32[]{:S(2)}) collective-permute-start(f32[16,32,128]{2,1,0:T(8,128)S(1)} %get-tuple-element.125), channel_id=1, source_target_pairs={{0,8},{4,12},{8,0},{12,4},{16,24},{20,28},{24,16},{28,20},{1,9},{5... | collective-permute-start | bytes 786440 | tf_op jit(solution)/shard_map/ppermute | solution.py:29
  205.9 24.8 %collective-permute-start.44 = (f32[4,16,32,128]{3,2,1,0:T(8,128)S(1)}, f32[4,16,32,128]{3,2,1,0:T(8,128)S(1)}, u32[]{:S(2)}, u32[]{:S(2)}) collective-permute-start(f32[4,16,32,128]{3,2,1,0:T(8,128)S(1)} %pack.35.refs_2_.refs_0_.refs_3_), channel_id=1, source_target_pairs={{0,2},{1,3},{2,0},{3,1},{4,6},{5,7},{6,4},{7,5},{8,10},{9,11},{10,... | collective-permute-start | bytes 3145736 | tf_op jit(solution)/shard_map/ppermute | solution.py:29
  208.6 22.1 %collective-permute-start.9 = (f32[16,32,128]{2,1,0:T(8,128)S(1)}, f32[16,32,128]{2,1,0:T(8,128)S(1)}, u32[]{:S(2)}, u32[]{:S(2)}) collective-permute-start(f32[16,32,128]{2,1,0:T(8,128)S(1)} %get-tuple-element.116), channel_id=1, source_target_pairs={{0,24},{4,28},{8,16},{12,20},{16,8},{20,12},{24,0},{28,4},{1,25},{... | collective-permute-start | bytes 786440 | tf_op jit(solution)/shard_map/ppermute | solution.py:29
  232.3 24.8 %collective-permute-start.46 = (f32[4,16,32,128]{3,2,1,0:T(8,128)S(1)}, f32[4,16,32,128]{3,2,1,0:T(8,128)S(1)}, u32[]{:S(2)}, u32[]{:S(2)}) collective-permute-start(f32[4,16,32,128]{3,2,1,0:T(8,128)S(1)} %pack.37.refs_2_.refs_0_.refs_4_), channel_id=1, source_target_pairs={{0,2},{1,3},{2,0},{3,1},{4,6},{5,7},{6,4},{7,5},{8,10},{9,11},{10,... | collective-permute-start | bytes 3145736 | tf_op jit(solution)/shard_map/ppermute | solution.py:29
  232.3 24.7 %collective-permute-start.5 = (f32[16,32,128]{2,1,0:T(8,128)S(1)}, f32[16,32,128]{2,1,0:T(8,128)S(1)}, u32[]{:S(2)}, u32[]{:S(2)}) collective-permute-start(f32[16,32,128]{2,1,0:T(8,128)S(1)} %get-tuple-element.111), channel_id=1, source_target_pairs={{0,24},{4,28},{8,16},{12,20},{16,8},{20,12},{24,0},{28,4},{1,25},{... | collective-permute-start | bytes 786440 | tf_op jit(solution)/shard_map/ppermute | solution.py:29
  233.8 23.3 %collective-permute-start.6 = (f32[16,32,128]{2,1,0:T(8,128)S(1)}, f32[16,32,128]{2,1,0:T(8,128)S(1)}, u32[]{:S(2)}, u32[]{:S(2)}) collective-permute-start(f32[16,32,128]{2,1,0:T(8,128)S(1)} %get-tuple-element.112), channel_id=1, source_target_pairs={{0,8},{4,12},{8,0},{12,4},{16,24},{20,28},{24,16},{28,20},{1,9},{5... | collective-permute-start | bytes 786440 | tf_op jit(solution)/shard_map/ppermute | solution.py:29
  258.7 20.3 %collective-permute-start.49 = (f32[3,16,32,128]{3,2,1,0:T(8,128)S(1)}, f32[3,16,32,128]{3,2,1,0:T(8,128)S(1)}, u32[]{:S(2)}, u32[]{:S(2)}) collective-permute-start(f32[3,16,32,128]{3,2,1,0:T(8,128)S(1)} %pack.39.refs_2_.refs_0_), channel_id=1, source_target_pairs={{0,1},{1,0},{2,3},{3,2},{4,5},{5,4},{6,7},{7,6},{8,9},{9,8},{10,11... | collective-permute-start | bytes 2359304 | tf_op jit(solution)/shard_map/ppermute | solution.py:29
  (75 other events, 665.3 us)
